TPU v7x, 32 devices: a whole 2x2x4 slice. The times are simulated.
32 devices in a mesh: grp: 2 (over y), pair: 4 (over z), aux: 2 (over x), sub: 2 (over core).
Axes of the slice: x: 2, y: 2, z: 4, core: 2. Of those that a mesh axis runs over, the one named last changes fastest.
Arguments:
- blocks: bfloat16 [32, 512, 512], P(('grp', 'pair'), 'aux', 'sub'), parts along dimension 0, may hold values from -0.75 to 0.75
- need_lists: int32 [8, 8], P('grp'), parts along dimension 0, may hold values from 0 to 15, as said below
- pair_slots: int32 [160, 2], P(('grp', 'pair')), parts along dimension 0, may hold values from 0 to 7
- pno_class: int32 [160], P(('grp', 'pair')), parts along dimension 0, may hold values from 0 to 2
- projection: bfloat16 [160, 512, 256], P(('grp', 'pair'), None, 'sub'), parts along dimension 0, may hold values from -0.25 to 0.25
- amplitudes: bfloat16 [160, 256, 256], P(('grp', 'pair'), 'sub', 'aux'), parts along dimension 0, may hold values from -1.1953125 to 1.1953125
- pno_energy: float32 [160, 256], P(('grp', 'pair')), parts along dimension 0, may hold values from 0.2 to 3
- occ_energy: float32 [32], P('grp'), parts along dimension 0, may hold values from -1.5 to -0.2
Outputs:
- residual: bfloat16 [160, 256, 256], P(('grp', 'pair'), 'sub', 'aux'), parts along dimension 0
There are 2 independent parts, one for each index of `grp`. A program takes and returns all parts, laid end to end along the dimension named above; each array names one. Nothing has to cross between parts.
Inputs may be any that keep to these rules, and one draw needn't show every extreme that they name: `need_lists`: row o lists 8 different orbitals; for each home h (orbitals h * 4 to h * 4 + 3) a row holds either none or exactly 2 of its orbitals.
All inputs are finite; a program needn't handle non-finite values.
Results may differ from a plain program's by a relative error of at most 0.0035.
Values may be sent and summed in bfloat16 or wider, within the bound.
A program may use at most 64 MiB of HBM per device.

v0:
```python
import jax
import jax.numpy as jnp
from jax import lax
from jax.sharding import PartitionSpec as P


def body(blocks, need_lists, pair_slots, pno_class, projection, amplitudes, pno_energy, occ_energy):
    owner = lax.axis_index("pair")
    wanted = lax.dynamic_index_in_dim(need_lists, owner, 0, keepdims=False)
    everything = lax.all_gather(blocks, "pair", axis=0, tiled=True)
    packed_pairs = jnp.take(everything, wanted, axis=0)
    whole = lax.all_gather(packed_pairs, "sub", axis=2, tiled=True)
    slot_i = pair_slots[:, 0]
    slot_j = pair_slots[:, 1]
    left_rows = jnp.take(whole, slot_i, axis=0)
    right_rows = jnp.take(whole, slot_j, axis=0)
    first_side = jnp.einsum(
        "ltb,lba->lta", left_rows, projection, preferred_element_type=jnp.float32
    ).astype(jnp.bfloat16)
    second_half = jnp.einsum(
        "ltb,lba->lta", right_rows, projection, preferred_element_type=jnp.float32
    ).astype(jnp.bfloat16)
    second_side = lax.all_gather(second_half, "sub", axis=2, tiled=True)
    summed = lax.psum_scatter(
        jnp.einsum("pqa,pqb->bpa", first_side, second_side, preferred_element_type=jnp.float32),
        "aux",
        scatter_dimension=0,
        tiled=True,
    )
    exchange_term = jnp.transpose(summed, (1, 2, 0))
    half_width = projection.shape[2]
    col_width = summed.shape[0]
    row_start = lax.axis_index("sub") * half_width
    col_start = lax.axis_index("aux") * col_width
    energy_rows = lax.dynamic_slice_in_dim(pno_energy, row_start, half_width, 1)
    energy_cols = lax.dynamic_slice_in_dim(pno_energy, col_start, col_width, 1)
    shift = jnp.take(occ_energy, jnp.take(wanted, slot_i)) + jnp.take(
        occ_energy, jnp.take(wanted, slot_j)
    )
    denominator = energy_rows[:, :, None] + energy_cols[:, None, :] - shift[:, None, None]
    npno = pno_energy.shape[1]
    live = npno // 4 * jnp.where(pno_class == 0, 1, jnp.where(pno_class == 1, 2, 4))
    row_mask_table = ((row_start + jnp.arange(half_width))[None, :] < live[:, None]).astype(
        jnp.float32
    )
    mask_cols = ((col_start + jnp.arange(col_width))[None, :] < live[:, None]).astype(jnp.float32)
    value = (
        row_mask_table[:, :, None]
        * mask_cols[:, None, :]
        * (exchange_term + denominator * amplitudes.astype(jnp.float32))
    )
    return value.astype(jnp.bfloat16)


def solution(mesh):
    placed = (
        P(("grp", "pair"), "aux", "sub"),
        P("grp", None),
        P(("grp", "pair"), None),
        P(("grp", "pair")),
        P(("grp", "pair"), None, "sub"),
        P(("grp", "pair"), "sub", "aux"),
        P(("grp", "pair"), None),
        P("grp"),
    )
    return jax.shard_map(
        body,
        mesh=mesh,
        in_specs=placed,
        out_specs=P(("grp", "pair"), "sub", "aux"),
        check_vma=False,
    )
```

profile of v0, /device:TPU:0, one launch (start us, length us, event | category | flops | bytes accessed | tf_op | source)
XLA Modules:
  0.0 153.1 jit_solution(18003654256020298354)
XLA Ops:
  6.5 0.0 copy-start
  6.5 0.0 all-gather.4.cloned.1.call-start
  6.5 0.7 all-gather.4.cloned.1.call-update
  7.3 0.0 all-gather.6.cloned.1.call-start
  7.3 0.7 fusion.20
  8.0 0.7 compare_and_fusion.2
  8.7 0.0 copy-start.3
  8.7 48.9 %all-gather.4.cloned.1.call-done = bf16[16,256,256]{2,1,0:T(8,128)(2,1)} async-done(((bf16[4,256,256]{2,1,0:T(8,128)(2,1)}), bf16[16,256,256]{2,1,0:T(8,128)(2,1)}) %all-gather.4.cloned.1.call-update) | async-done | bytes 2097168 | tf_op jit(solution)/shard_map/all_gather | solution.py:10
  57.6 3.2 %gather_fusion = bf16[8,256,256]{2,1,0:T(8,128)(2,1)} fusion(bf16[16,256,256]{2,1,0:T(8,128)(2,1)} %all-gather.4.cloned.1.call-done, s32[1024]{0:T(1024)S(1)} %pad_clamp_fusion.4), kind=kCustom, calls=%fused_computation.6 | custom fusion | bytes 2097184 | tf_op jit(solution)/shard_map/jit(_take)/gather | solution.py:11
  60.8 2.4 %broadcast_select_fusion = bf16[8,256,256]{2,1,0:T(8,128)(2,1)} fusion(bf16[8,256,256]{2,1,0:T(8,128)(2,1)} %gather_fusion, pred[8]{0:T(512)(128)(4,1)S(1)} %get-tuple-element.12), kind=kLoop, calls=%fused_computation.21 | loop fusion | flops 524288 | bytes 2097160 | tf_op jit(solution)/shard_map/jit(_take)/select_n | solution.py:11
  63.2 0.0 all-gather.6.cloned.1.call-update
  63.2 0.0 all-gather.8.cloned.1.call-start
  63.2 0.0 copy-done.3
  63.3 9.1 %all-gather.6.cloned.1.call-done = bf16[8,256,512]{2,1,0:T(8,128)(2,1)} async-done(((bf16[8,256,256]{2,1,0:T(8,128)(2,1)}), bf16[8,256,512]{2,1,0:T(8,128)(2,1)}) %all-gather.6.cloned.1.call-update) | async-done | bytes 2097168 | tf_op jit(solution)/shard_map/all_gather | solution.py:12
  72.4 5.6 %gather_fusion.1 = bf16[20,256,512]{2,1,0:T(8,128)(2,1)} fusion(bf16[8,256,512]{2,1,0:T(8,128)(2,1)} %all-gather.6.cloned.1.call-done, s32[1024]{0:T(1024)S(1)} %pad_clamp_fusion.3), kind=kCustom, calls=%fused_computation.clone | custom fusion | bytes 10485840 | tf_op jit(solution)/shard_map/jit(_take)/gather | solution.py:16
  78.0 5.1 %fusion.8 = bf16[20,256,128]{2,1,0:T(8,128)(2,1)} fusion(bf16[20,512,128]{2,1,0:T(8,128)(2,1)S(1)} %copy-done, bf16[20,256,512]{2,1,0:T(8,128)(2,1)} %gather_fusion.1, pred[20]{0:T(512)(128)(4,1)S(1)} %get-tuple-element.16), kind=kOutput, calls=%fused_computation.16 | convolution fusion | flops 674365440 | bytes 9175060 | tf_op jit(solution)/shard_map/ltb,lba->lta/dot_general | solution.py:20
  83.1 0.0 all-gather.8.cloned.1.call-update
  83.1 0.0 reduce-scatter.2.cloned.1.call-start
  83.2 5.7 %gather_fusion.2 = bf16[20,256,512]{2,1,0:T(8,128)(2,1)} fusion(bf16[8,256,512]{2,1,0:T(8,128)(2,1)} %all-gather.6.cloned.1.call-done, s32[1024]{0:T(1024)S(1)} %pad_clamp_fusion.2), kind=kCustom, calls=%fused_computation.3.clone | custom fusion | bytes 10485840 | tf_op jit(solution)/shard_map/jit(_take)/gather | solution.py:15
  88.9 6.6 %all-gather.8.cloned.1.call-done = bf16[20,256,256]{2,1,0:T(8,128)(2,1)} async-done(((bf16[20,256,128]{2,1,0:T(8,128)(2,1)}), bf16[20,256,256]{2,1,0:T(8,128)(2,1)}) %all-gather.8.cloned.1.call-update) | async-done | bytes 2621456 | tf_op jit(solution)/shard_map/all_gather | solution.py:23
  95.5 7.2 %convolution_bitcast_fusion = f32[256,20,128]{2,0,1:T(8,128)} fusion(bf16[20,256,256]{2,1,0:T(8,128)(2,1)} %all-gather.8.cloned.1.call-done, bf16[20,512,128]{2,1,0:T(8,128)(2,1)S(1)} %copy-done, bf16[20,256,512]{2,1,0:T(8,128)(2,1)} %gather_fusion.2, pred[20]{0:T(512)(128)(4,1)S(1)} %get-tuple-element.6), kind=kOutput, calls=%fused_computation.15 | convolution fusion | flops 1009909760 | bytes 13107220 | tf_op jit(solution)/shard_map/pqa,pqb->bpa/dot_general | solution.py:25
  102.7 0.0 reduce-scatter.2.cloned.1.call-update
  102.7 0.7 gather_fusion.5
  103.4 0.7 gather_fusion.3
  104.2 0.7 gather_fusion.4
  104.9 0.7 gather_fusion.6
  105.6 1.4 copy.14
  107.0 0.0 copy-done.4
  107.1 0.1 compare_convert_fusion.1
  107.1 34.5 %reduce-scatter.2.cloned.1.call-done = f32[128,20,128]{2,0,1:T(8,128)} async-done(((f32[256,20,128]{2,0,1:T(8,128)}), f32[128,20,128]{2,0,1:T(8,128)}) %reduce-scatter.2.cloned.1.call-update) | async-done | bytes 1310736 | tf_op jit(solution)/shard_map/reduce_scatter | solution.py:24
  141.7 2.8 %fusion.17 = bf16[20,128,128]{1,2,0:T(8,128)(2,1)} fusion(f32[128,20,128]{2,0,1:T(8,128)} %reduce-scatter.2.cloned.1.call-done, bf16[20,128,128]{1,2,0:T(8,128)(2,1)S(1)} %copy.14, f32[20]{0:T(128)S(1)} %fusion.19, f32[20,128]{1,0:T(8,128)S(1)} %get-tuple-element.15, f32[20,128]{1,0:T(8,128)S(1)} %get-tuple-element.14, f32[20,128]{1,0:T(8,128)S(1)} %get-tuple-element.19, ...), kind=kLoop, calls=%fused_computation.20 | loop fusion | flops 2621440 | bytes 2662480 | tf_op jit(solution)/shard_map/convert_element_type | solution.py:52
  144.4 2.2 %copy.15 = bf16[20,128,128]{2,1,0:T(8,128)(2,1)} copy(bf16[20,128,128]{1,2,0:T(8,128)(2,1)} %fusion.17) | data formatting | bytes 1310720 | tf_op jit(solution)/shard_map/convert_element_type | solution.py:52
  (17 shorter events, 0.1 us)
Async XLA Ops:
  6.5 71.5 %copy-start = (bf16[20,512,128]{2,1,0:T(8,128)(2,1)S(1)}, bf16[20,512,128]{2,1,0:T(8,128)(2,1)}, u32[]{:S(2)}) copy-start(bf16[20,512,128]{2,1,0:T(8,128)(2,1)} %param.18) | copy-start | bytes 7864324
  6.5 51.1 %all-gather.4.cloned.1.call-start = ((), (), s32[]{:S(2)}) async-start(), calls=%async_computation.1 | async-start | bytes 2621440 | tf_op jit(solution)/shard_map/all_gather | solution.py:10
  7.3 65.1 %all-gather.6.cloned.1.call-start = ((), (), s32[]{:S(2)}) async-start(), calls=%async_computation.2 | async-start | bytes 3145728 | tf_op jit(solution)/shard_map/all_gather | solution.py:12
  8.7 54.5 %copy-start.3 = (s32[20,2]{0,1:T(2,128)S(1)}, s32[20,2]{0,1:T(2,128)}, u32[]{:S(2)}) copy-start(s32[20,2]{0,1:T(2,128)} %param.16) | copy-start | bytes 484
  63.2 32.3 %all-gather.8.cloned.1.call-start = ((), (), s32[]{:S(2)}) async-start(), calls=%async_computation.3 | async-start | bytes 3932160 | tf_op jit(solution)/shard_map/all_gather | solution.py:23
  83.1 58.5 %reduce-scatter.2.cloned.1.call-start = ((), (), s32[]{:S(2)}) async-start(), calls=%async_computation.4 | async-start | bytes 3932160 | tf_op jit(solution)/shard_map/reduce_scatter | solution.py:24
  102.7 1.5 copy-start.1
  102.7 4.3 %copy-start.2 = (f32[20,256]{1,0:T(8,128)S(1)}, f32[20,256]{1,0:T(8,128)}, u32[]{:S(2)}) copy-start(f32[20,256]{1,0:T(8,128)} %param.20) | copy-start | bytes 61444
  102.7 4.3 %copy-start.4 = (s32[20]{0:T(128)S(1)}, s32[20]{0:T(128)}, u32[]{:S(2)}) copy-start(s32[20]{0:T(128)} %param.17) | copy-start | bytes 244
Sparse Core Ops, SparseCore 0:
  8.9 48.6 all-gather.3
  63.3 9.0 all-gather.5
  83.3 12.2 all-gather.7
  102.8 38.7 reduce-scatter.1
where the time goes:
time: 154 us; the launch traced here: 153 us
  waiting for transfers between devices  99.9 us (65%)
  local copies, waits for them, and re-layouts  20.9 us (14%)
  between operations  13.3 us (9%)
  matrix products  12.3 us (8%)
  other arithmetic  6.69 us (4%)
    all_gather x1, waiting for transfers between devices, body(): everything = lax.all_gather(blocks, 'pair', axis=0, tiled=True)  48.9 us
    reduce_scatter x1, waiting for transfers between devices, body(): lax.psum_scatter(jnp.einsum('pqa,pqb->bpa', first_side, second_side, pref...  34.5 us
    all_gather x1, waiting for transfers between devices, body(): whole = lax.all_gather(packed_pairs, 'sub', axis=2, tiled=True)  9.1 us
    dot_general x1, matrix products, body(): jnp.einsum('pqa,pqb->bpa', first_side, second_side, preferred_element_typ...  7.16 us
    all_gather x1, waiting for transfers between devices, body(): second_side = lax.all_gather(second_half, 'sub', axis=2, tiled=True)  6.64 us
    gather x1, local copies, waits for them, and re-layouts, body(): left_rows = jnp.take(whole, slot_i, axis=0)  5.67 us
    gather x1, local copies, waits for them, and re-layouts, body(): right_rows = jnp.take(whole, slot_j, axis=0)  5.63 us
    dot_general x1, matrix products, body(): jnp.einsum('ltb,lba->lta', right_rows, projection, preferred_element_type...  5.11 us
  transfers between devices with their start and end apart: 4, of which 4 were waited for; matrix products, arithmetic and copies ran while one was open for 7% of the time, Pallas kernels for 0%

commit v1 on v0

--- a/solution.py
+++ b/solution.py
@@ -1,6 +1,10 @@
+import functools
+
 import jax
 import jax.numpy as jnp
 from jax import lax
+from jax.experimental import pallas as pl
+from jax.experimental.pallas import tpu as pltpu
 from jax.sharding import PartitionSpec as P
 
 
@@ -52,7 +56,298 @@
     return value.astype(jnp.bfloat16)
 
 
+CHUNKS = 4
+MESH = pl.DeviceIdType.MESH
+
+
+def kernel(
+    n_pair,
+    blocks_ref,
+    need_ref,
+    slots_ref,
+    class_ref,
+    proj_ref,
+    amp_ref,
+    energy_ref,
+    occ_ref,
+    out_ref,
+    *scratch,
+):
+    n_chunk = CHUNKS
+    whole = scratch[:n_chunk]
+    (packed, p_sub, p_aux, amp, acc, table, z_send, z_recv, x_send, x_recv, c_send, c_recv,
+     d_send, d_recv, p_sem, l_sem) = scratch[n_chunk:]
+    home = lax.axis_index("pair")
+    x = lax.axis_index("aux")
+    c = lax.axis_index("sub")
+    per_home, q_dev, half_mu = blocks_ref.shape
+    need = need_ref.shape[1]
+    rows = q_dev // n_chunk
+    n_occ = amp.shape[0]
+    width = out_ref.shape[2]
+
+    load_p = pltpu.make_async_copy(proj_ref, p_sub, l_sem.at[0])
+    load_amp = pltpu.make_async_copy(amp_ref, amp, l_sem.at[1])
+    load_aux = pltpu.make_async_copy(proj_ref, p_aux, l_sem.at[2])
+    load_p.start()
+    load_amp.start()
+
+    barrier = pltpu.get_barrier_semaphore()
+    for off in range(1, n_pair):
+        pl.semaphore_signal(
+            barrier, inc=1, device_id={"pair": lax.rem(home + off, n_pair)}, device_id_type=MESH
+        )
+    pl.semaphore_signal(barrier, inc=1, device_id={"aux": 1 - x}, device_id_type=MESH)
+    pl.semaphore_signal(barrier, inc=1, device_id={"sub": 1 - c}, device_id_type=MESH)
+
+    def pack(owner, store):
+        seen = jnp.int32(0)
+        local = [jnp.int32(0), jnp.int32(0)]
+        for s in range(need):
+            orbital = need_ref[owner, s] - home * per_home
+            here = jnp.logical_and(orbital >= 0, orbital < per_home)
+            for k in range(2):
+                local[k] = jnp.where(jnp.logical_and(here, seen == k), orbital, local[k])
+            seen = seen + here.astype(jnp.int32)
+        for t in range(n_chunk):
+            for k in range(2):
+                store(t, k, blocks_ref[local[k], pl.ds(t * rows, rows), :])
+
+    for off in range(1, n_pair):
+        def store(t, k, value, off=off):
+            packed[off - 1, t, k] = value
+        pack(lax.rem(home + off, n_pair), store)
+
+    pl.semaphore_wait(barrier, n_pair + 1)
+
+    def z_copy(t, off):
+        return pltpu.make_async_remote_copy(
+            src_ref=packed.at[off - 1, t],
+            dst_ref=whole[t].at[c, pl.ds(home * 2, 2), x],
+            send_sem=z_send.at[t, off - 1],
+            recv_sem=z_recv.at[t, home],
+            device_id={"pair": lax.rem(home + off, n_pair)},
+            device_id_type=MESH,
+        )
+
+    def z_wait(t, off):
+        source = lax.rem(home + n_pair - off, n_pair)
+        place = whole[t].at[c, pl.ds(source * 2, 2), x]
+        pltpu.make_async_remote_copy(
+            src_ref=place,
+            dst_ref=place,
+            send_sem=z_send.at[t, off - 1],
+            recv_sem=z_recv.at[t, source],
+            device_id={"pair": source},
+            device_id_type=MESH,
+        ).wait_recv()
+
+    def hop(t, off, axis, to, half, send, recv, core):
+        source = lax.rem(home + n_pair - off, n_pair)
+        place = whole[t].at[core, pl.ds(source * 2, 2), half]
+        return pltpu.make_async_remote_copy(
+            src_ref=place,
+            dst_ref=place,
+            send_sem=send.at[t, source],
+            recv_sem=recv.at[t, source],
+            device_id={axis: to},
+            device_id_type=MESH,
+        )
+
+    def x_out(t, off):
+        return hop(t, off, "aux", 1 - x, x, x_send, x_recv, c)
+
+    def x_in(t, off):
+        return hop(t, off, "aux", 1 - x, 1 - x, x_send, x_recv, c)
+
+    def c_out(t, off):
+        return hop(t, off, "sub", 1 - c, x, c_send, c_recv, c)
+
+    def c_in(t, off):
+        return hop(t, off, "sub", 1 - c, x, c_send, c_recv, 1 - c)
+
+    def d_out(t, off):
+        return hop(t, off, "sub", 1 - c, 1 - x, d_send, d_recv, c)
+
+    def d_in(t, off):
+        return hop(t, off, "sub", 1 - c, 1 - x, d_send, d_recv, 1 - c)
+
+    for t in range(n_chunk):
+        for off in range(1, n_pair):
+            z_copy(t, off).start()
+
+    def store_own(t, k, value):
+        whole[t][c, home * 2 + k, x] = value
+
+    pack(home, store_own)
+    for t in range(n_chunk):
+        x_out(t, 0).start()
+        c_out(t, 0).start()
+
+    send_p = pltpu.make_async_remote_copy(
+        src_ref=proj_ref,
+        dst_ref=p_aux,
+        send_sem=p_sem.at[0],
+        recv_sem=p_sem.at[1],
+        device_id={"sub": 1 - c},
+        device_id_type=MESH,
+    )
+
+    @pl.when(x == c)
+    def _():
+        send_p.start()
+        load_aux.start()
+
+    for s in range(need):
+        orbital = need_ref[home, s]
+        origin = lax.div(orbital, jnp.int32(per_home))
+        rank = jnp.int32(0)
+        for before in range(s):
+            rank = rank + (lax.div(need_ref[home, before], jnp.int32(per_home)) == origin).astype(jnp.int32)
+        table[s] = origin * 2 + jnp.minimum(rank, 1)
+
+    load_amp.wait()
+
+    for i in range(n_occ):
+        low, high = energy_ref[i : i + 1, :width], energy_ref[i : i + 1, width:]
+        e_rows = jnp.where(c == 0, low, high)
+        e_cols = jnp.where(x == 0, low, high)
+        shift = occ_ref[need_ref[home, slots_ref[i, 0]]] + occ_ref[need_ref[home, slots_ref[i, 1]]]
+        e_rows = jnp.transpose(jnp.broadcast_to(e_rows, (width, width)))
+        acc[i] = (e_rows + e_cols - shift) * amp[i].astype(jnp.float32)
+
+    load_p.wait()
+
+    @pl.when(x == c)
+    def _():
+        send_p.wait_send()
+        load_aux.wait()
+
+    @pl.when(x != c)
+    def _():
+        send_p.wait_recv()
+
+    group = 4 if n_occ % 4 == 0 else 1
+
+    def side(t, slot, basis, i):
+        total = None
+        for core in range(2):
+            left = whole[t][core, slot].reshape(2 * rows, half_mu)
+            part = jnp.dot(
+                left, basis[i, core * half_mu : (core + 1) * half_mu], preferred_element_type=jnp.float32
+            )
+            total = part if total is None else total + part
+        return total.astype(jnp.bfloat16)
+
+    def compute(t):
+        def step(g, carry):
+            for u in range(group):
+                i = g * group + u
+                first = side(t, table[slots_ref[i, 0]], p_sub, i)
+                second = side(t, table[slots_ref[i, 1]], p_aux, i)
+                value = acc[i] + lax.dot_general(
+                    first, second, (((0,), (0,)), ((), ())), preferred_element_type=jnp.float32
+                )
+                if t < n_chunk - 1:
+                    acc[i] = value
+                else:
+                    size = class_ref[i]
+                    live = jnp.where(size == 0, width // 2, jnp.where(size == 1, width, 2 * width))
+                    a = lax.broadcasted_iota(jnp.int32, (width, width), 0) + c * width
+                    b = lax.broadcasted_iota(jnp.int32, (width, width), 1) + x * width
+                    keep = jnp.logical_and(a < live, b < live)
+                    out_ref[i] = jnp.where(keep, value, 0.0).astype(out_ref.dtype)
+            return carry
+
+        lax.fori_loop(0, n_occ // group, step, 0)
+
+    def arrived(t):
+        for off in range(n_pair):
+            c_in(t, off).wait_recv()
+            d_in(t, off).wait_recv()
+
+    for t in range(n_chunk):
+        for off in range(n_pair):
+            if off:
+                z_wait(t, off)
+                x_out(t, off).start()
+                c_out(t, off).start()
+            if t:
+                x_in(t - 1, off).wait_recv()
+                d_out(t - 1, off).start()
+        if t:
+            arrived(t - 1)
+            compute(t - 1)
+    for off in range(n_pair):
+        x_in(n_chunk - 1, off).wait_recv()
+        d_out(n_chunk - 1, off).start()
+    arrived(n_chunk - 1)
+    compute(n_chunk - 1)
+
+    for t in range(n_chunk):
+        for off in range(n_pair):
+            if off:
+                z_copy(t, off).wait_send()
+            x_out(t, off).wait_send()
+            c_out(t, off).wait_send()
+            d_out(t, off).wait_send()
+
+
+def gathered(n_pair, blocks, need_lists, pair_slots, pno_class, projection, amplitudes, pno_energy, occ_energy):
+    per_home, q_dev, half_mu = blocks.shape
+    n_occ, mu, width = projection.shape
+    rows = q_dev // CHUNKS
+    dma = pltpu.SemaphoreType.DMA
+    vmem = pl.BlockSpec(memory_space=pltpu.VMEM)
+    smem = pl.BlockSpec(memory_space=pltpu.SMEM)
+    hbm = pl.BlockSpec(memory_space=pl.ANY)
+    scratch = [pltpu.VMEM((2, 2 * n_pair, 2, rows, half_mu), jnp.bfloat16) for _ in range(CHUNKS)]
+    scratch += [
+        pltpu.VMEM((n_pair - 1, CHUNKS, 2, rows, half_mu), jnp.bfloat16),
+        pltpu.VMEM((n_occ, mu, width), jnp.bfloat16),
+        pltpu.VMEM((n_occ, mu, width), jnp.bfloat16),
+        pltpu.VMEM(amplitudes.shape, jnp.bfloat16),
+        pltpu.VMEM(amplitudes.shape, jnp.float32),
+        pltpu.SMEM((need_lists.shape[1],), jnp.int32),
+        dma((CHUNKS, n_pair - 1)),
+        dma((CHUNKS, n_pair)),
+    ]
+    scratch += [dma((CHUNKS, n_pair)) for _ in range(6)]
+    scratch += [dma((2,)), dma((3,))]
+    flops = 2 * n_occ * (2 * 2 * q_dev * mu * width + 2 * q_dev * width * width)
+    return pl.pallas_call(
+        functools.partial(kernel, n_pair),
+        out_shape=jax.ShapeDtypeStruct(amplitudes.shape, jnp.bfloat16),
+        in_specs=[vmem, smem, smem, smem, hbm, hbm, vmem, smem],
+        out_specs=vmem,
+        scratch_shapes=scratch,
+        compiler_params=pltpu.CompilerParams(
+            collective_id=0, has_side_effects=True, vmem_limit_bytes=40 * 1024 * 1024
+        ),
+        cost_estimate=pl.CostEstimate(flops=flops, bytes_accessed=8 * 1024 * 1024, transcendentals=0),
+    )(blocks, need_lists, pair_slots, pno_class, projection, amplitudes, pno_energy, occ_energy)
+
+
+def fits(mesh, blocks, need_lists, projection, amplitudes):
+    n_pair = mesh.shape["pair"]
+    if mesh.shape["aux"] != 2 or mesh.shape["sub"] != 2 or n_pair < 2:
+        return False
+    per_home, q_dev, half_mu = blocks.shape
+    width = projection.shape[2]
+    if amplitudes.shape[1:] != (width, width) or width % 128 or half_mu % 128 or q_dev % (16 * CHUNKS):
+        return False
+    held = 4 * 2 * n_pair * q_dev * half_mu * 2
+    held += 2 * n_pair * q_dev * half_mu * 2 + 2 * projection.size * 2 + amplitudes.size * 10
+    return held < 24 * 1024 * 1024
+
+
 def solution(mesh):
+    def one_device(blocks, need_lists, pair_slots, pno_class, projection, amplitudes, pno_energy, occ_energy):
+        args = (blocks, need_lists, pair_slots, pno_class, projection, amplitudes, pno_energy, occ_energy)
+        if fits(mesh, blocks, need_lists, projection, amplitudes):
+            return gathered(mesh.shape["pair"], *args)
+        return body(*args)
+
     placed = (
         P(("grp", "pair"), "aux", "sub"),
         P("grp", None),
@@ -64,7 +359,7 @@
         P("grp"),
     )
     return jax.shard_map(
-        body,
+        one_device,
         mesh=mesh,
         in_specs=placed,
         out_specs=P(("grp", "pair"), "sub", "aux"),

time: 154 us -> 58 us (0.38)
  waiting for transfers between devices: 99.9 us -> 0 us
  Pallas kernels: 0 us -> 49.5 us
  between operations: 13.3 us -> 0.02 us
  local copies, waits for them, and re-layouts: 20.9 us -> 8.2 us
  matrix products: 12.3 us -> 0 us
  other arithmetic: 6.69 us -> 0 us
    all_gather x3 -> x0, waiting for transfers between devices: 64.6 us -> none  [the longest x1 48.9 us: body(): everything = lax.all_gather(blocks, 'pair', axis=0, tiled=True)]
    pallas_call x0 -> x1, Pallas kernels: none -> 49.5 us  [gathered(): pl.pallas_call(functools.partial(kernel, n_pair), out_shape=jax.ShapeDtyp...]
    reduce_scatter x1 -> x0, waiting for transfers between devices: 34.5 us -> none  [body(): lax.psum_scatter(jnp.einsum('pqa,pqb->bpa', first_side, second_side, pref...]
    gather x7 -> x0, local copies, waits for them, and re-layouts: 17.3 us -> none  [the longest x1 5.67 us: body(): left_rows = jnp.take(whole, slot_i, axis=0)]
    dot_general x2 -> x0, matrix products: 12.3 us -> none  [the longest x1 7.16 us: body(): jnp.einsum('pqa,pqb->bpa', first_side, second_side, preferred_element_typ...]
    unnamed x11 -> x16, local copies, waits for them, and re-layouts: 1.44 us -> 8.2 us
    select_n x3 -> x0, other arithmetic: 3.1 us -> none  [the longest x2 3.09 us: body(): packed_pairs = jnp.take(everything, wanted, axis=0)]
    convert_element_type x2 -> x0, other arithmetic: 2.84 us -> none  [the longest x1 2.77 us: body(): return value.astype(jnp.bfloat16)]
  transfers between devices with their start and end apart: 4 -> 0, of which waited for: 4 -> 0; matrix products, arithmetic and copies ran while one was open for 7% -> 0% of each run, Pallas kernels for 0% -> 0%
where the time goes in v1:
time: 58 us; the launch traced here: 57.7 us
  Pallas kernels  49.5 us (85%)
  local copies, waits for them, and re-layouts  8.2 us (14%)
    pallas_call x1, Pallas kernels, gathered(): pl.pallas_call(functools.partial(kernel, n_pair), out_shape=jax.ShapeDtyp...  49.5 us
    unnamed x16, local copies, waits for them, and re-layouts  8.2 us

profile of v1, /device:TPU:0, one launch (start us, length us, event | category | flops | bytes accessed | tf_op | source)
XLA Modules:
  0.0 57.7 jit_solution(3840911657340691991)
XLA Ops:
  0.0 0.8 %copy.9.slots_ref = s32[20,2]{1,0:T(8,128)S(1)} copy(s32[20,2]{0,1:T(2,128)} %param.10) | data formatting | bytes 320 | tf_op args[2]
  0.8 0.0 copy-start
  0.8 1.7 %copy-done = bf16[20,512,128]{2,1,0:T(8,128)(2,1)S(1)} copy-done((bf16[20,512,128]{2,1,0:T(8,128)(2,1)S(1)}, bf16[20,512,128]{2,1,0:T(8,128)(2,1)}, u32[]{:S(2)}) %copy-start) | copy-done | bytes 2621464
  2.5 0.0 copy-start.1
  2.5 1.1 %copy-done.1 = bf16[20,128,128]{2,1,0:T(8,128)(2,1)S(1)} copy-done((bf16[20,128,128]{2,1,0:T(8,128)(2,1)S(1)}, bf16[20,128,128]{2,1,0:T(8,128)(2,1)}, u32[]{:S(2)}) %copy-start.1) | copy-done | bytes 655384
  3.6 0.0 copy-start.2
  3.6 1.0 %copy-done.2 = bf16[4,256,256]{2,1,0:T(8,128)(2,1)S(1)} copy-done((bf16[4,256,256]{2,1,0:T(8,128)(2,1)S(1)}, bf16[4,256,256]{2,1,0:T(8,128)(2,1)}, u32[]{:S(2)}) %copy-start.2) | copy-done | bytes 524312
  4.6 0.0 copy-start.3
  4.6 0.7 %copy-done.3 = f32[20,256]{1,0:T(8,128)S(1)} copy-done((f32[20,256]{1,0:T(8,128)S(1)}, f32[20,256]{1,0:T(8,128)}, u32[]{:S(2)}) %copy-start.3) | copy-done | bytes 20504
  5.4 0.0 copy-start.4
  5.4 0.7 %copy-done.4 = s32[4,8]{1,0:T(4,128)S(1)} copy-done((s32[4,8]{1,0:T(4,128)S(1)}, s32[4,8]{1,0:T(4,128)}, u32[]{:S(2)}) %copy-start.4) | copy-done | bytes 152
  6.1 0.0 copy-start.5
  6.1 0.7 %copy-done.5 = s32[20]{0:T(128)S(1)} copy-done((s32[20]{0:T(128)S(1)}, s32[20]{0:T(128)}, u32[]{:S(2)}) %copy-start.5) | copy-done | bytes 104
  6.7 0.0 copy-start.6
  6.7 0.7 %copy-done.6 = f32[16]{0:T(128)S(1)} copy-done((f32[16]{0:T(128)S(1)}, f32[16]{0:T(128)}, u32[]{:S(2)}) %copy-start.6) | copy-done | bytes 88
  7.4 49.5 %shard_map.82 = bf16[20,128,128]{2,1,0:T(8,128)(2,1)S(1)} custom-call(bf16[4,256,256]{2,1,0:T(8,128)(2,1)S(1)} %copy-done.2, s32[4,8]{1,0:T(4,128)S(1)} %copy-done.4, s32[20,2]{1,0:T(8,128)S(1)} %copy.9.slots_ref, s32[20]{0:T(128)S(1)} %copy-done.5, bf16[20,512,128]{2,1,0:T(8,128)(2,1)S(1)} %copy-done, bf16[20,128,128]{2,1,0:T(8,128)(2,1)S(1)} %copy-done.1, ...), custom_call_target="tpu_custom_call" | custom-call | flops 3019898880 | bytes 8388608 | tf_op jit(solution)/shard_map/pallas_call | solution.py:318
  56.8 0.8 %copy.11 = bf16[20,128,128]{2,1,0:T(8,128)(2,1)} copy(bf16[20,128,128]{2,1,0:T(8,128)(2,1)S(1)} %shard_map.82) | data formatting | bytes 1310720
Async XLA Ops:
  0.8 1.7 %copy-start = (bf16[20,512,128]{2,1,0:T(8,128)(2,1)S(1)}, bf16[20,512,128]{2,1,0:T(8,128)(2,1)}, u32[]{:S(2)}) copy-start(bf16[20,512,128]{2,1,0:T(8,128)(2,1)} %proj_ref.1) | copy-start | bytes 7864324
  2.5 1.1 %copy-start.1 = (bf16[20,128,128]{2,1,0:T(8,128)(2,1)S(1)}, bf16[20,128,128]{2,1,0:T(8,128)(2,1)}, u32[]{:S(2)}) copy-start(bf16[20,128,128]{2,1,0:T(8,128)(2,1)} %amp_ref.1) | copy-start | bytes 1966084
  3.6 1.0 %copy-start.2 = (bf16[4,256,256]{2,1,0:T(8,128)(2,1)S(1)}, bf16[4,256,256]{2,1,0:T(8,128)(2,1)}, u32[]{:S(2)}) copy-start(bf16[4,256,256]{2,1,0:T(8,128)(2,1)} %blocks_ref.1) | copy-start | bytes 1572868
  4.6 0.7 %copy-start.3 = (f32[20,256]{1,0:T(8,128)S(1)}, f32[20,256]{1,0:T(8,128)}, u32[]{:S(2)}) copy-start(f32[20,256]{1,0:T(8,128)} %energy_ref.1) | copy-start | bytes 61444
  5.4 0.7 %copy-start.4 = (s32[4,8]{1,0:T(4,128)S(1)}, s32[4,8]{1,0:T(4,128)}, u32[]{:S(2)}) copy-start(s32[4,8]{1,0:T(4,128)} %need_ref.1) | copy-start | bytes 388
  6.1 0.7 %copy-start.5 = (s32[20]{0:T(128)S(1)}, s32[20]{0:T(128)}, u32[]{:S(2)}) copy-start(s32[20]{0:T(128)} %class_ref.1) | copy-start | bytes 244
  6.7 0.7 %copy-start.6 = (f32[16]{0:T(128)S(1)}, f32[16]{0:T(128)}, u32[]{:S(2)}) copy-start(f32[16]{0:T(128)} %occ_ref.1) | copy-start | bytes 196

commit v2 on v1

--- a/solution.py
+++ b/solution.py
@@ -56,41 +56,39 @@
     return value.astype(jnp.bfloat16)
 
 
-CHUNKS = 4
+CHUNKS = 2
 MESH = pl.DeviceIdType.MESH
 
 
 def kernel(
     n_pair,
-    blocks_ref,
-    need_ref,
-    slots_ref,
-    class_ref,
+    blocks_hbm,
+    need_hbm,
+    slots_hbm,
+    class_hbm,
     proj_ref,
     amp_ref,
-    energy_ref,
-    occ_ref,
+    energy_hbm,
+    occ_hbm,
     out_ref,
     *scratch,
 ):
     n_chunk = CHUNKS
     whole = scratch[:n_chunk]
-    (packed, p_sub, p_aux, amp, acc, table, z_send, z_recv, x_send, x_recv, c_send, c_recv,
-     d_send, d_recv, p_sem, l_sem) = scratch[n_chunk:]
+    (blocks_ref, need_ref, slots_ref, class_ref, energy_ref, occ_ref, packed, basis, amp, acc,
+     result, table, z_send, z_recv, x_send, x_recv, c_send, c_recv, d_send, d_recv, s_sem,
+     l_sem, o_sem) = scratch[n_chunk:]
     home = lax.axis_index("pair")
     x = lax.axis_index("aux")
     c = lax.axis_index("sub")
     per_home, q_dev, half_mu = blocks_ref.shape
     need = need_ref.shape[1]
     rows = q_dev // n_chunk
-    n_occ = amp.shape[0]
+    n_mine = basis.shape[0]
     width = out_ref.shape[2]
-
-    load_p = pltpu.make_async_copy(proj_ref, p_sub, l_sem.at[0])
-    load_amp = pltpu.make_async_copy(amp_ref, amp, l_sem.at[1])
-    load_aux = pltpu.make_async_copy(proj_ref, p_aux, l_sem.at[2])
-    load_p.start()
-    load_amp.start()
+    mine = c * n_mine
+    theirs = (1 - c) * n_mine
+    here_cols = pl.ds(pl.multiple_of(c * width, width), width)
 
     barrier = pltpu.get_barrier_semaphore()
     for off in range(1, n_pair):
@@ -99,6 +97,26 @@
         )
     pl.semaphore_signal(barrier, inc=1, device_id={"aux": 1 - x}, device_id_type=MESH)
     pl.semaphore_signal(barrier, inc=1, device_id={"sub": 1 - c}, device_id_type=MESH)
+
+    loads = [
+        pltpu.make_async_copy(source, target, l_sem.at[n])
+        for n, (source, target) in enumerate(
+            [
+                (need_hbm, need_ref),
+                (blocks_hbm, blocks_ref),
+                (slots_hbm, slots_ref),
+                (class_hbm, class_ref),
+                (occ_hbm, occ_ref),
+                (energy_hbm, energy_ref),
+                (amp_ref.at[pl.ds(mine, n_mine)], amp.at[:, here_cols]),
+                (proj_ref.at[pl.ds(mine, n_mine)], basis.at[:, :, here_cols]),
+            ]
+        )
+    ]
+    for load in loads:
+        load.start()
+    loads[0].wait()
+    loads[1].wait()
 
     def pack(owner, store):
         seen = jnp.int32(0)
@@ -118,6 +136,11 @@
             packed[off - 1, t, k] = value
         pack(lax.rem(home + off, n_pair), store)
 
+    def store_own(t, k, value):
+        whole[t][c, home * 2 + k, x] = value
+
+    pack(home, store_own)
+
     pl.semaphore_wait(barrier, n_pair + 1)
 
     def z_copy(t, off):
@@ -172,31 +195,28 @@
     def d_in(t, off):
         return hop(t, off, "sub", 1 - c, 1 - x, d_send, d_recv, 1 - c)
 
+    def swap(n, source, target):
+        return pltpu.make_async_remote_copy(
+            src_ref=source,
+            dst_ref=target,
+            send_sem=s_sem.at[n, 0],
+            recv_sem=s_sem.at[n, 1],
+            device_id={"sub": 1 - c},
+            device_id_type=MESH,
+        )
+
     for t in range(n_chunk):
         for off in range(1, n_pair):
             z_copy(t, off).start()
-
-    def store_own(t, k, value):
-        whole[t][c, home * 2 + k, x] = value
-
-    pack(home, store_own)
+        x_out(t, 0).start()
+    swaps = [
+        swap(0, amp_ref.at[pl.ds(theirs, n_mine)], amp.at[:, here_cols]),
+        swap(1, proj_ref.at[pl.ds(theirs, n_mine)], basis.at[:, :, here_cols]),
+    ]
+    for copy in swaps:
+        copy.start()
     for t in range(n_chunk):
-        x_out(t, 0).start()
         c_out(t, 0).start()
-
-    send_p = pltpu.make_async_remote_copy(
-        src_ref=proj_ref,
-        dst_ref=p_aux,
-        send_sem=p_sem.at[0],
-        recv_sem=p_sem.at[1],
-        device_id={"sub": 1 - c},
-        device_id_type=MESH,
-    )
-
-    @pl.when(x == c)
-    def _():
-        send_p.start()
-        load_aux.start()
 
     for s in range(need):
         orbital = need_ref[home, s]
@@ -206,60 +226,96 @@
             rank = rank + (lax.div(need_ref[home, before], jnp.int32(per_home)) == origin).astype(jnp.int32)
         table[s] = origin * 2 + jnp.minimum(rank, 1)
 
-    load_amp.wait()
-
-    for i in range(n_occ):
-        low, high = energy_ref[i : i + 1, :width], energy_ref[i : i + 1, width:]
-        e_rows = jnp.where(c == 0, low, high)
-        e_cols = jnp.where(x == 0, low, high)
-        shift = occ_ref[need_ref[home, slots_ref[i, 0]]] + occ_ref[need_ref[home, slots_ref[i, 1]]]
-        e_rows = jnp.transpose(jnp.broadcast_to(e_rows, (width, width)))
-        acc[i] = (e_rows + e_cols - shift) * amp[i].astype(jnp.float32)
-
-    load_p.wait()
-
-    @pl.when(x == c)
-    def _():
-        send_p.wait_send()
-        load_aux.wait()
-
-    @pl.when(x != c)
-    def _():
-        send_p.wait_recv()
-
-    group = 4 if n_occ % 4 == 0 else 1
-
-    def side(t, slot, basis, i):
+    for load in loads[2:]:
+        load.wait()
+    for copy in swaps:
+        copy.wait()
+
+    for i in range(n_mine):
+        p = mine + i
+        energy = jnp.where(c == 0, energy_ref[i : i + 1, :], energy_ref[n_mine + i : n_mine + i + 1, :])
+        cols = jnp.where(x == 0, energy[:, :width], energy[:, width:])
+        shift = occ_ref[need_ref[home, slots_ref[0, p]]] + occ_ref[need_ref[home, slots_ref[1, p]]]
+        for half in range(2):
+            part = slice(half * width, (half + 1) * width)
+            down = jnp.transpose(jnp.broadcast_to(energy[:, part], (width, width)))
+            acc[i, part] = (down + cols - shift) * amp[i, part].astype(jnp.float32)
+
+    group = 2 if n_mine % 2 == 0 else 1
+
+    def compute(t, i):
+        p = mine + i
+        slot_i = table[slots_ref[0, p]]
+        slot_j = table[slots_ref[1, p]]
         total = None
         for core in range(2):
-            left = whole[t][core, slot].reshape(2 * rows, half_mu)
+            left = jnp.concatenate(
+                [
+                    whole[t][core, slot_i].reshape(2 * rows, half_mu),
+                    whole[t][core, slot_j].reshape(2 * rows, half_mu),
+                ],
+                axis=0,
+            )
             part = jnp.dot(
                 left, basis[i, core * half_mu : (core + 1) * half_mu], preferred_element_type=jnp.float32
             )
             total = part if total is None else total + part
-        return total.astype(jnp.bfloat16)
-
-    def compute(t):
+        first = total[: 2 * rows].astype(jnp.bfloat16)
+        second = total[2 * rows :]
+        second = jnp.where(x == 0, second[:, :width], second[:, width:]).astype(jnp.bfloat16)
+        value = acc[i] + lax.dot_general(
+            first, second, (((0,), (0,)), ((), ())), preferred_element_type=jnp.float32
+        )
+        if t < n_chunk - 1:
+            acc[i] = value
+            return
+        size = class_ref[p]
+        live = jnp.where(size == 0, width // 2, jnp.where(size == 1, width, 2 * width))
+        a = lax.broadcasted_iota(jnp.int32, value.shape, 0)
+        b = lax.broadcasted_iota(jnp.int32, value.shape, 1) + x * width
+        keep = jnp.logical_and(a < live, b < live)
+        value = jnp.where(keep, value, 0.0).astype(out_ref.dtype)
+        result[i, 0] = value[:width]
+        result[i, 1] = value[width:]
+
+    def keep_rows(g):
+        return pltpu.make_async_copy(
+            result.at[pl.ds(g * group, group), c],
+            out_ref.at[pl.ds(mine + g * group, group)],
+            o_sem.at[0, g],
+        )
+
+    def give_rows(g):
+        return pltpu.make_async_remote_copy(
+            src_ref=result.at[pl.ds(g * group, group), 1 - c],
+            dst_ref=out_ref.at[pl.ds(mine + g * group, group)],
+            send_sem=o_sem.at[1, g],
+            recv_sem=o_sem.at[2, g],
+            device_id={"sub": 1 - c},
+            device_id_type=MESH,
+        )
+
+    def take_rows(g):
+        place = out_ref.at[pl.ds(theirs + g * group, group)]
+        return pltpu.make_async_remote_copy(
+            src_ref=place,
+            dst_ref=place,
+            send_sem=o_sem.at[1, g],
+            recv_sem=o_sem.at[2, g],
+            device_id={"sub": 1 - c},
+            device_id_type=MESH,
+        )
+
+    def compute_all(t):
         def step(g, carry):
             for u in range(group):
-                i = g * group + u
-                first = side(t, table[slots_ref[i, 0]], p_sub, i)
-                second = side(t, table[slots_ref[i, 1]], p_aux, i)
-                value = acc[i] + lax.dot_general(
-                    first, second, (((0,), (0,)), ((), ())), preferred_element_type=jnp.float32
-                )
-                if t < n_chunk - 1:
-                    acc[i] = value
-                else:
-                    size = class_ref[i]
-                    live = jnp.where(size == 0, width // 2, jnp.where(size == 1, width, 2 * width))
-                    a = lax.broadcasted_iota(jnp.int32, (width, width), 0) + c * width
-                    b = lax.broadcasted_iota(jnp.int32, (width, width), 1) + x * width
-                    keep = jnp.logical_and(a < live, b < live)
-                    out_ref[i] = jnp.where(keep, value, 0.0).astype(out_ref.dtype)
+                compute(t, g * group + u)
+            if t == n_chunk - 1:
+                keep_rows(g).start()
+                give_rows(g).start()
             return carry
 
-        lax.fori_loop(0, n_occ // group, step, 0)
+        lax.fori_loop(0, n_mine // group, step, 0)
 
     def arrived(t):
         for off in range(n_pair):
@@ -277,12 +333,12 @@
                 d_out(t - 1, off).start()
         if t:
             arrived(t - 1)
-            compute(t - 1)
+            compute_all(t - 1)
     for off in range(n_pair):
         x_in(n_chunk - 1, off).wait_recv()
         d_out(n_chunk - 1, off).start()
     arrived(n_chunk - 1)
-    compute(n_chunk - 1)
+    compute_all(n_chunk - 1)
 
     for t in range(n_chunk):
         for off in range(n_pair):
@@ -291,6 +347,10 @@
             x_out(t, off).wait_send()
             c_out(t, off).wait_send()
             d_out(t, off).wait_send()
+    for g in range(n_mine // group):
+        keep_rows(g).wait()
+        give_rows(g).wait_send()
+        take_rows(g).wait_recv()
 
 
 def gathered(n_pair, blocks, need_lists, pair_slots, pno_class, projection, amplitudes, pno_energy, occ_energy):
@@ -298,34 +358,39 @@
     n_occ, mu, width = projection.shape
     rows = q_dev // CHUNKS
     dma = pltpu.SemaphoreType.DMA
-    vmem = pl.BlockSpec(memory_space=pltpu.VMEM)
-    smem = pl.BlockSpec(memory_space=pltpu.SMEM)
-    hbm = pl.BlockSpec(memory_space=pl.ANY)
+    hbm = pl.BlockSpec(memory_space=pltpu.HBM)
     scratch = [pltpu.VMEM((2, 2 * n_pair, 2, rows, half_mu), jnp.bfloat16) for _ in range(CHUNKS)]
+    n_mine = n_occ // 2
     scratch += [
+        pltpu.VMEM(blocks.shape, blocks.dtype),
+        pltpu.SMEM(need_lists.shape, jnp.int32),
+        pltpu.SMEM(pair_slots.shape[::-1], jnp.int32),
+        pltpu.SMEM(pno_class.shape, jnp.int32),
+        pltpu.VMEM(pno_energy.shape, jnp.float32),
+        pltpu.SMEM(occ_energy.shape, jnp.float32),
         pltpu.VMEM((n_pair - 1, CHUNKS, 2, rows, half_mu), jnp.bfloat16),
-        pltpu.VMEM((n_occ, mu, width), jnp.bfloat16),
-        pltpu.VMEM((n_occ, mu, width), jnp.bfloat16),
-        pltpu.VMEM(amplitudes.shape, jnp.bfloat16),
-        pltpu.VMEM(amplitudes.shape, jnp.float32),
+        pltpu.VMEM((n_mine, mu, 2 * width), jnp.bfloat16),
+        pltpu.VMEM((n_mine, 2 * width, width), jnp.bfloat16),
+        pltpu.VMEM((n_mine, 2 * width, width), jnp.float32),
+        pltpu.VMEM((n_mine, 2, width, width), jnp.bfloat16),
         pltpu.SMEM((need_lists.shape[1],), jnp.int32),
         dma((CHUNKS, n_pair - 1)),
         dma((CHUNKS, n_pair)),
     ]
     scratch += [dma((CHUNKS, n_pair)) for _ in range(6)]
-    scratch += [dma((2,)), dma((3,))]
+    scratch += [dma((2, 2)), dma((8,)), dma((3, n_mine))]
     flops = 2 * n_occ * (2 * 2 * q_dev * mu * width + 2 * q_dev * width * width)
     return pl.pallas_call(
         functools.partial(kernel, n_pair),
         out_shape=jax.ShapeDtypeStruct(amplitudes.shape, jnp.bfloat16),
-        in_specs=[vmem, smem, smem, smem, hbm, hbm, vmem, smem],
-        out_specs=vmem,
+        in_specs=[hbm] * 8,
+        out_specs=hbm,
         scratch_shapes=scratch,
         compiler_params=pltpu.CompilerParams(
-            collective_id=0, has_side_effects=True, vmem_limit_bytes=40 * 1024 * 1024
+            collective_id=0, has_side_effects=True, vmem_limit_bytes=60 * 1024 * 1024
         ),
         cost_estimate=pl.CostEstimate(flops=flops, bytes_accessed=8 * 1024 * 1024, transcendentals=0),
-    )(blocks, need_lists, pair_slots, pno_class, projection, amplitudes, pno_energy, occ_energy)
+    )(blocks, need_lists, jnp.transpose(pair_slots), pno_class, projection, amplitudes, pno_energy, occ_energy)
 
 
 def fits(mesh, blocks, need_lists, projection, amplitudes):
@@ -334,7 +399,7 @@
         return False
     per_home, q_dev, half_mu = blocks.shape
     width = projection.shape[2]
-    if amplitudes.shape[1:] != (width, width) or width % 128 or half_mu % 128 or q_dev % (16 * CHUNKS):
+    if amplitudes.shape[1:] != (width, width) or width % 128 or half_mu % 128 or q_dev % (16 * CHUNKS) or amplitudes.shape[0] % 2:
         return False
     held = 4 * 2 * n_pair * q_dev * half_mu * 2
     held += 2 * n_pair * q_dev * half_mu * 2 + 2 * projection.size * 2 + amplitudes.size * 10

time: 58 us -> 45.4 us (0.78)
  Pallas kernels: 49.5 us -> 42.7 us
  local copies, waits for them, and re-layouts: 8.2 us -> 1.99 us
    pallas_call x1, Pallas kernels: 49.5 us -> 42.7 us  [gathered(): pl.pallas_call(functools.partial(kernel, n_pair), out_shape=jax.ShapeDtyp...]
    unnamed x16 -> x1, local copies, waits for them, and re-layouts: 8.2 us -> 1.99 us
where the time goes in v2:
time: 45.4 us; the launch traced here: 44.7 us
  Pallas kernels  42.7 us (94%)
  local copies, waits for them, and re-layouts  1.99 us (4%)
    pallas_call x1, Pallas kernels, gathered(): pl.pallas_call(functools.partial(kernel, n_pair), out_shape=jax.ShapeDtyp...  42.7 us
    unnamed x1, local copies, waits for them, and re-layouts  1.99 us

profile of v2, /device:TPU:0, one launch (start us, length us, event | category | flops | bytes accessed | tf_op | source)
XLA Modules:
  0.0 44.7 jit_solution(8001060274791248724)
XLA Ops:
  0.0 42.7 %shard_map.82 = bf16[20,128,128]{2,1,0:T(8,128)(2,1)} custom-call(bf16[4,256,256]{2,1,0:T(8,128)(2,1)} %blocks_hbm.1, s32[4,8]{1,0:T(4,128)} %need_hbm.1, s32[2,20]{1,0:T(2,128)} %bitcast.1, s32[20]{0:T(128)} %class_hbm.1, bf16[20,512,128]{2,1,0:T(8,128)(2,1)} %proj_ref.1, bf16[20,128,128]{2,1,0:T(8,128)(2,1)} %amp_ref.1, f32[20,256]{1,0:T(8,128)} %energy_hbm.1, ...), custom_call_target="tpu_custom_call" | custom-call | flops 3019898880 | bytes 8388608 | tf_op jit(solution)/shard_map/pallas_call | solution.py:383
  42.7 2.0 %copy.10 = bf16[20,128,128]{2,1,0:T(8,128)(2,1)} copy(bf16[20,128,128]{2,1,0:T(8,128)(2,1)} %shard_map.82) | data formatting | bytes 1310720

commit v3 on v2

--- a/solution.py
+++ b/solution.py
@@ -56,7 +56,7 @@
     return value.astype(jnp.bfloat16)
 
 
-CHUNKS = 2
+SPLIT = (8, 8)
 MESH = pl.DeviceIdType.MESH
 
 
@@ -73,7 +73,7 @@
     out_ref,
     *scratch,
 ):
-    n_chunk = CHUNKS
+    n_chunk = len(SPLIT)
     whole = scratch[:n_chunk]
     (blocks_ref, need_ref, slots_ref, class_ref, energy_ref, occ_ref, packed, basis, amp, acc,
      result, table, z_send, z_recv, x_send, x_recv, c_send, c_recv, d_send, d_recv, s_sem,
@@ -83,17 +83,26 @@
     c = lax.axis_index("sub")
     per_home, q_dev, half_mu = blocks_ref.shape
     need = need_ref.shape[1]
-    rows = q_dev // n_chunk
+    unit = q_dev // 16
+    size = [part * unit for part in SPLIT]
+    begin = [sum(size[:t]) for t in range(n_chunk)]
     n_mine = basis.shape[0]
     width = out_ref.shape[2]
     mine = c * n_mine
     theirs = (1 - c) * n_mine
     here_cols = pl.ds(pl.multiple_of(c * width, width), width)
 
+    def partner(off):
+        place, bit = 0, 1
+        while bit < n_pair:
+            place = place + lax.rem(lax.div(home, bit) + off // bit, 2) * bit
+            bit *= 2
+        return place
+
     barrier = pltpu.get_barrier_semaphore()
     for off in range(1, n_pair):
         pl.semaphore_signal(
-            barrier, inc=1, device_id={"pair": lax.rem(home + off, n_pair)}, device_id_type=MESH
+            barrier, inc=1, device_id={"pair": partner(off)}, device_id_type=MESH
         )
     pl.semaphore_signal(barrier, inc=1, device_id={"aux": 1 - x}, device_id_type=MESH)
     pl.semaphore_signal(barrier, inc=1, device_id={"sub": 1 - c}, device_id_type=MESH)
@@ -127,17 +136,17 @@
             for k in range(2):
                 local[k] = jnp.where(jnp.logical_and(here, seen == k), orbital, local[k])
             seen = seen + here.astype(jnp.int32)
+        for k in range(2):
+            store(k, local[k])
+
+    for off in range(1, n_pair):
+        def store(k, index, off=off):
+            packed[off - 1, k] = blocks_ref[index]
+        pack(partner(off), store)
+
+    def store_own(k, index):
         for t in range(n_chunk):
-            for k in range(2):
-                store(t, k, blocks_ref[local[k], pl.ds(t * rows, rows), :])
-
-    for off in range(1, n_pair):
-        def store(t, k, value, off=off):
-            packed[off - 1, t, k] = value
-        pack(lax.rem(home + off, n_pair), store)
-
-    def store_own(t, k, value):
-        whole[t][c, home * 2 + k, x] = value
+            whole[t][c, home * 2 + k, x] = blocks_ref[index, begin[t] : begin[t] + size[t], :]
 
     pack(home, store_own)
 
@@ -145,16 +154,16 @@
 
     def z_copy(t, off):
         return pltpu.make_async_remote_copy(
-            src_ref=packed.at[off - 1, t],
+            src_ref=packed.at[off - 1, :, pl.ds(begin[t], size[t])],
             dst_ref=whole[t].at[c, pl.ds(home * 2, 2), x],
             send_sem=z_send.at[t, off - 1],
             recv_sem=z_recv.at[t, home],
-            device_id={"pair": lax.rem(home + off, n_pair)},
+            device_id={"pair": partner(off)},
             device_id_type=MESH,
         )
 
     def z_wait(t, off):
-        source = lax.rem(home + n_pair - off, n_pair)
+        source = partner(off)
         place = whole[t].at[c, pl.ds(source * 2, 2), x]
         pltpu.make_async_remote_copy(
             src_ref=place,
@@ -166,7 +175,7 @@
         ).wait_recv()
 
     def hop(t, off, axis, to, half, send, recv, core):
-        source = lax.rem(home + n_pair - off, n_pair)
+        source = partner(off)
         place = whole[t].at[core, pl.ds(source * 2, 2), half]
         return pltpu.make_async_remote_copy(
             src_ref=place,
@@ -206,8 +215,11 @@
         )
 
     for t in range(n_chunk):
-        for off in range(1, n_pair):
+        z_copy(t, 1).start()
+    for t in range(n_chunk):
+        for off in range(2, n_pair):
             z_copy(t, off).start()
+    for t in range(n_chunk):
         x_out(t, 0).start()
     swaps = [
         swap(0, amp_ref.at[pl.ds(theirs, n_mine)], amp.at[:, here_cols]),
@@ -241,25 +253,23 @@
             down = jnp.transpose(jnp.broadcast_to(energy[:, part], (width, width)))
             acc[i, part] = (down + cols - shift) * amp[i, part].astype(jnp.float32)
 
-    group = 2 if n_mine % 2 == 0 else 1
+    group = 5 if n_mine % 5 == 0 else 1
 
     def compute(t, i):
         p = mine + i
         slot_i = table[slots_ref[0, p]]
         slot_j = table[slots_ref[1, p]]
-        total = None
-        for core in range(2):
-            left = jnp.concatenate(
-                [
-                    whole[t][core, slot_i].reshape(2 * rows, half_mu),
-                    whole[t][core, slot_j].reshape(2 * rows, half_mu),
-                ],
-                axis=0,
-            )
-            part = jnp.dot(
-                left, basis[i, core * half_mu : (core + 1) * half_mu], preferred_element_type=jnp.float32
-            )
-            total = part if total is None else total + part
+        rows = size[t]
+        left = jnp.concatenate(
+            [
+                jnp.concatenate(
+                    [whole[t][core, slot].reshape(2 * rows, half_mu) for core in range(2)], axis=1
+                )
+                for slot in (slot_i, slot_j)
+            ],
+            axis=0,
+        )
+        total = jnp.dot(left, basis[i], preferred_element_type=jnp.float32)
         first = total[: 2 * rows].astype(jnp.bfloat16)
         second = total[2 * rows :]
         second = jnp.where(x == 0, second[:, :width], second[:, width:]).astype(jnp.bfloat16)
@@ -269,8 +279,8 @@
         if t < n_chunk - 1:
             acc[i] = value
             return
-        size = class_ref[p]
-        live = jnp.where(size == 0, width // 2, jnp.where(size == 1, width, 2 * width))
+        kind = class_ref[p]
+        live = jnp.where(kind == 0, width // 2, jnp.where(kind == 1, width, 2 * width))
         a = lax.broadcasted_iota(jnp.int32, value.shape, 0)
         b = lax.broadcasted_iota(jnp.int32, value.shape, 1) + x * width
         keep = jnp.logical_and(a < live, b < live)
@@ -323,8 +333,12 @@
             d_in(t, off).wait_recv()
 
     for t in range(n_chunk):
+        z_wait(t, 1)
+        x_out(t, 1).start()
+        c_out(t, 1).start()
+    for t in range(n_chunk):
         for off in range(n_pair):
-            if off:
+            if off > 1:
                 z_wait(t, off)
                 x_out(t, off).start()
                 c_out(t, off).start()
@@ -356,10 +370,10 @@
 def gathered(n_pair, blocks, need_lists, pair_slots, pno_class, projection, amplitudes, pno_energy, occ_energy):
     per_home, q_dev, half_mu = blocks.shape
     n_occ, mu, width = projection.shape
-    rows = q_dev // CHUNKS
+    unit = q_dev // 16
     dma = pltpu.SemaphoreType.DMA
     hbm = pl.BlockSpec(memory_space=pltpu.HBM)
-    scratch = [pltpu.VMEM((2, 2 * n_pair, 2, rows, half_mu), jnp.bfloat16) for _ in range(CHUNKS)]
+    scratch = [pltpu.VMEM((2, 2 * n_pair, 2, part * unit, half_mu), jnp.bfloat16) for part in SPLIT]
     n_mine = n_occ // 2
     scratch += [
         pltpu.VMEM(blocks.shape, blocks.dtype),
@@ -368,16 +382,16 @@
         pltpu.SMEM(pno_class.shape, jnp.int32),
         pltpu.VMEM(pno_energy.shape, jnp.float32),
         pltpu.SMEM(occ_energy.shape, jnp.float32),
-        pltpu.VMEM((n_pair - 1, CHUNKS, 2, rows, half_mu), jnp.bfloat16),
+        pltpu.VMEM((n_pair - 1, 2, q_dev, half_mu), jnp.bfloat16),
         pltpu.VMEM((n_mine, mu, 2 * width), jnp.bfloat16),
         pltpu.VMEM((n_mine, 2 * width, width), jnp.bfloat16),
         pltpu.VMEM((n_mine, 2 * width, width), jnp.float32),
         pltpu.VMEM((n_mine, 2, width, width), jnp.bfloat16),
         pltpu.SMEM((need_lists.shape[1],), jnp.int32),
-        dma((CHUNKS, n_pair - 1)),
-        dma((CHUNKS, n_pair)),
+        dma((len(SPLIT), n_pair - 1)),
+        dma((len(SPLIT), n_pair)),
     ]
-    scratch += [dma((CHUNKS, n_pair)) for _ in range(6)]
+    scratch += [dma((len(SPLIT), n_pair)) for _ in range(6)]
     scratch += [dma((2, 2)), dma((8,)), dma((3, n_mine))]
     flops = 2 * n_occ * (2 * 2 * q_dev * mu * width + 2 * q_dev * width * width)
     return pl.pallas_call(
@@ -395,11 +409,11 @@
 
 def fits(mesh, blocks, need_lists, projection, amplitudes):
     n_pair = mesh.shape["pair"]
-    if mesh.shape["aux"] != 2 or mesh.shape["sub"] != 2 or n_pair < 2:
+    if mesh.shape["aux"] != 2 or mesh.shape["sub"] != 2 or n_pair < 2 or n_pair & (n_pair - 1):
         return False
     per_home, q_dev, half_mu = blocks.shape
     width = projection.shape[2]
-    if amplitudes.shape[1:] != (width, width) or width % 128 or half_mu % 128 or q_dev % (16 * CHUNKS) or amplitudes.shape[0] % 2:
+    if amplitudes.shape[1:] != (width, width) or width % 128 or half_mu % 128 or q_dev % 256 or amplitudes.shape[0] % 2:
         return False
     held = 4 * 2 * n_pair * q_dev * half_mu * 2
     held += 2 * n_pair * q_dev * half_mu * 2 + 2 * projection.size * 2 + amplitudes.size * 10

time: 45.4 us -> 43.1 us (0.949); the launches traced: 44.7 us -> 42.9 us
  Pallas kernels: 42.7 us -> 40.9 us
    pallas_call x1, Pallas kernels: 42.7 us -> 40.9 us  [gathered(): pl.pallas_call(functools.partial(kernel, n_pair), out_shape=jax.ShapeDtyp...]
where the time goes in v3:
time: 43.1 us; the launch traced here: 42.9 us
  Pallas kernels  40.9 us (95%)
  local copies, waits for them, and re-layouts  1.99 us (5%)
    pallas_call x1, Pallas kernels, gathered(): pl.pallas_call(functools.partial(kernel, n_pair), out_shape=jax.ShapeDtyp...  40.9 us
    unnamed x1, local copies, waits for them, and re-layouts  1.99 us

profile of v3, /device:TPU:0, one launch (start us, length us, event | category | flops | bytes accessed | tf_op | source)
XLA Modules:
  0.0 42.9 jit_solution(4297746296052612473)
XLA Ops:
  0.0 40.9 %shard_map.82 = bf16[20,128,128]{2,1,0:T(8,128)(2,1)} custom-call(bf16[4,256,256]{2,1,0:T(8,128)(2,1)} %blocks_hbm.1, s32[4,8]{1,0:T(4,128)} %need_hbm.1, s32[2,20]{1,0:T(2,128)} %bitcast.1, s32[20]{0:T(128)} %class_hbm.1, bf16[20,512,128]{2,1,0:T(8,128)(2,1)} %proj_ref.1, bf16[20,128,128]{2,1,0:T(8,128)(2,1)} %amp_ref.1, f32[20,256]{1,0:T(8,128)} %energy_hbm.1, ...), custom_call_target="tpu_custom_call" | custom-call | flops 3019898880 | bytes 8388608 | tf_op jit(solution)/shard_map/pallas_call | solution.py:397
  41.0 2.0 %copy.10 = bf16[20,128,128]{2,1,0:T(8,128)(2,1)} copy(bf16[20,128,128]{2,1,0:T(8,128)(2,1)} %shard_map.82) | data formatting | bytes 1310720
